TPU v7x, 32 devices: a whole 2x2x4 slice. The times are simulated.
32 devices in a mesh: gx: 8 (over z, y), gy: 2 (over x), gz: 2 (over core).
Axes of the slice: x: 2, y: 2, z: 4, core: 2. Of those that a mesh axis runs over, the one named last changes fastest.
Arguments:
- pops: float32 [19, 32, 64, 256], P(None, 'gz', 'gx', 'gy'), as said below
- solid: int32 [32, 64, 256], P('gz', 'gx', 'gy'), may hold values 0 or 1
- surf_cell: int32 [2, 8, 2, 512], P('gz', 'gx', 'gy'), may hold values from 0 to 16383
- surf_panel: int32 [2, 8, 2, 512], P('gz', 'gx', 'gy'), may hold values from -1 to 39, as said below
- surf_area: float32 [2, 8, 2, 512], P('gz', 'gx', 'gy'), may hold values from 0.1 to 1
- mode_shape: float32 [2, 8, 2, 12, 512], P('gz', 'gx', 'gy'), may hold values from -5 to 5
- mode_of_panel: int32 [40], replicated, may hold values from 0 to 11
- compliance: float32 [12], replicated, may hold values from 0.3 to 3
Outputs:
- read: float32 [19, 32, 64, 256], P(None, 'gz', 'gx', 'gy')
- panel_force: float32 [40], replicated
- mode_amplitude: float32 [12], replicated
Inputs may be any that keep to these rules, and one draw needn't show every extreme that they name: pops is positive, with densities near 1 and flow speeds below 0.25. `surf_panel`: -1 marks an empty slot; on each device the live slots come first, at least 64 of them; some device has all 512 slots live; one panel's surfels lie on at most about 40 consecutive bricks in the linear order (vertical, streamwise, crosswise) of the devices, counted periodically so that the last brick is followed by the first.
All inputs are finite; a program needn't handle non-finite values. No bound on the sum of `solid` on one device may be relied on, other than what follows from the above.
Results may differ from a plain program's by a relative error of at most 0.00011.
Values sent between devices are 32-bit elements; how exact they have to be, the bound alone decides.
A program may use at most 64 MiB of HBM per device.

v0:
```python
import jax
import jax.numpy as jnp
from jax import lax
from jax.sharding import PartitionSpec as P

PANELS = 40
MODES = 12
VELOCITY = (
    (0, 0, 0),
    (1, 0, 0),
    (-1, 0, 0),
    (0, 1, 0),
    (0, -1, 0),
    (0, 0, 1),
    (0, 0, -1),
    (1, 1, 0),
    (-1, -1, 0),
    (1, -1, 0),
    (-1, 1, 0),
    (1, 0, 1),
    (-1, 0, -1),
    (1, 0, -1),
    (-1, 0, 1),
    (0, 1, 1),
    (0, -1, -1),
    (0, 1, -1),
    (0, -1, 1),
)
WEIGHTS = (1.0 / 3.0,) + (1.0 / 18.0,) * 6 + (1.0 / 36.0,) * 12
OPPOSITE = (0, 2, 1, 4, 3, 6, 5, 8, 7, 10, 9, 12, 11, 14, 13, 16, 15, 18, 17)
OMEGA = 1.0 / 0.6
WALL_SCALE = 0.02


def padded_2(block, sides, width):
    for axis, dim in sides:
        count = lax.axis_size(axis)
        forward = [(i, i + 1) for i in range(count - 1)]
        forward.append((count - 1, 0))
        backward = [(target, source) for source, target in forward]
        low = lax.ppermute(
            lax.slice_in_dim(block, block.shape[dim] - width, None, axis=dim), axis, forward
        )
        high = lax.ppermute(lax.slice_in_dim(block, 0, width, axis=dim), axis, backward)
        block = jnp.concatenate([low, block, high], axis=dim)
    return block


def collide(pops, solid):
    density = pops[0]
    for index in range(1, 19):
        density = density + pops[index]
    moments = []
    for axis in range(3):
        total = jnp.zeros_like(density)
        for index in range(19):
            comp = VELOCITY[index][axis]
            if comp == 1:
                total = total + pops[index]
            elif comp == -1:
                total = total - pops[index]
        moments.append(total / density)
    squared = moments[0] * moments[0] + moments[1] * moments[1] + moments[2] * moments[2]
    result = []
    for index in range(19):
        projected = jnp.zeros_like(density)
        for axis in range(3):
            comp = VELOCITY[index][axis]
            if comp == 1:
                projected = projected + moments[axis]
            elif comp == -1:
                projected = projected - moments[axis]
        equilib = (
            WEIGHTS[index]
            * density
            * (1.0 + 3.0 * projected + 4.5 * projected * projected - 1.5 * squared)
        )
        relaxed = pops[index] + OMEGA * (equilib - pops[index])
        result.append(jnp.where(solid == 1, pops[OPPOSITE[index]], relaxed))
    return (density, result)


def stream_joint(pieces):
    field = jnp.stack(pieces)
    depth, rows, width = (field.shape[1], field.shape[2], field.shape[3])
    padded = padded_2(field, (("gx", 2), ("gy", 3), ("gz", 1)), 1)
    result = []
    for index in range(19):
        vel = VELOCITY[index]
        result.append(
            padded[
                index,
                1 - vel[2] : 1 - vel[2] + depth,
                1 - vel[0] : 1 - vel[0] + rows,
                1 - vel[1] : 1 - vel[1] + width,
            ]
        )
    return result


def stream_all(pieces):
    return stream_joint(pieces)


def per_device(
    pops, solid, surf_cell, surf_panel, surf_area, mode_shape, mode_of_panel, compliance
):
    depth, rows, width = (pops.shape[1], pops.shape[2], pops.shape[3])
    density, post = collide(pops, solid)
    flat_density = density.reshape(-1)
    cell_list = surf_cell.reshape(-1)
    panel_list = surf_panel.reshape(-1)
    gathered = flat_density[cell_list]
    live = panel_list >= 0
    contrib = jnp.where(live, surf_area.reshape(-1) * ((gathered - 1.0) / 3.0), 0.0)
    panel_ids = jnp.arange(PANELS, dtype=jnp.int32)
    partial_force = jnp.sum(
        jnp.where(panel_list[:, None] == panel_ids[None, :], contrib[:, None], 0.0), axis=0
    )
    panel_force = lax.psum(partial_force, ("gx", "gy", "gz"))
    mode_ids = jnp.arange(MODES, dtype=jnp.int32)
    mode_load = jnp.sum(
        jnp.where(mode_of_panel[:, None] == mode_ids[None, :], panel_force[:, None], 0.0), axis=0
    )
    mode_amplitude = compliance * mode_load
    shapes = mode_shape.reshape(MODES, -1)
    wall = WALL_SCALE * jnp.sum(mode_amplitude[:, None] * shapes, axis=0)
    values = jnp.where(live, gathered * wall, 0.0)
    wall_flux = jnp.zeros_like(flat_density).at[cell_list].add(values).reshape(depth, rows, width)
    corrected = []
    for index in range(19):
        coef = 6.0 * WEIGHTS[index] * VELOCITY[index][0]
        corrected.append(post[index] + coef * wall_flux)
    result = stream_all(corrected)
    return (jnp.stack(result), panel_force, mode_amplitude)


def solution(mesh):
    placed = (
        P(None, "gz", "gx", "gy"),
        P("gz", "gx", "gy"),
        P("gz", "gx", "gy", None),
        P("gz", "gx", "gy", None),
        P("gz", "gx", "gy", None),
        P("gz", "gx", "gy", None, None),
        P(),
        P(),
    )
    return jax.shard_map(
        per_device,
        mesh=mesh,
        in_specs=placed,
        out_specs=(P(None, "gz", "gx", "gy"), P(), P()),
        check_vma=False,
    )
```

profile of v0, /device:TPU:0, one launch (start us, length us, event | category | flops | bytes accessed | tf_op | source)
XLA Modules:
  0.0 97.8 jit_solution(2532107182724770170)
XLA Ops:
  0.6 0.7 compare_select_fusion
  1.3 1.4 %bitcast_add_fusion = f32[16384]{0:T(1024)S(1)} fusion(f32[19,16,8,128]{3,2,1,0:T(8,128)} %param.8), kind=kLoop, calls=%fused_computation.249 | loop fusion | flops 294912 | bytes 1310720 | tf_op jit(solution)/shard_map/add | solution.py:52
  2.7 0.0 copy-start.6
  2.7 0.0 copy-start.7
  2.7 0.0 copy-start.9
  2.7 0.0 copy-start.10
  2.7 0.0 copy-start.5
  2.8 0.0 copy-start.2
  2.8 0.0 copy-start.4
  2.8 3.1 %gather_fusion = f32[512]{0:T(512)S(1)} fusion(f32[16384]{0:T(1024)S(1)} %bitcast_add_fusion, s32[1024]{0:T(1024)S(1)} %pad_clamp_fusion), kind=kCustom, calls=%fused_computation | custom fusion | bytes 6144 | tf_op jit(solution)/shard_map/gather | solution.py:113
  5.9 0.0 copy-done.6
  5.9 0.0 copy-done.7
  6.0 0.1 select_reduce_fusion
  6.1 42.0 %psum.7 = f32[40]{0:T(128)S(1)} all-reduce(f32[40]{0:T(128)S(1)} %select_reduce_fusion), channel_id=1, replica_groups=mesh['gx'=8,'gy'=2,'gz'=2] {'gx','gy','gz'}, use_global_device_ids=true, to_apply=%region_1.2 | all-reduce | flops 40 | bytes 320 | tf_op jit(solution)/shard_map/psum | solution.py:120
  48.1 0.0 copy-done.9
  48.1 0.1 select_reduce_fusion.1
  48.2 0.0 copy-done.5
  48.2 0.0 copy-start.8
  48.3 0.1 fusion.168
  48.4 3.3 %scatter_custom_fusion = f32[16384]{0:T(1024)S(1)} fusion(s32[512]{0:T(512)S(1)} %bitcast.409, f32[512]{0:T(512)S(1)} %multiply_select_fusion, f32[]{:T(128)} %constant.4.clone.1), kind=kCustom, calls=%fused_computation.305 | custom fusion | flops 512 | bytes 65540 | tf_op jit(solution)/shard_map/scatter-add | solution.py:129
  51.6 0.0 copy-done.2
  51.7 0.0 copy-done.4
  51.7 0.2 fusion.1
  51.9 0.1 copy.82
  52.9 0.2 fusion.175
  53.1 2.3 %collective-permute-start = (f32[19,16,1,128]{3,1,2,0:T(8,128)S(1)}, f32[19,16,1,128]{3,1,2,0:T(8,128)S(1)}, u32[]{:S(2)}, u32[]{:S(2)}) collective-permute-start(f32[19,16,1,128]{3,1,2,0:T(8,128)S(1)} %bitcast.405), channel_id=1, source_target_pairs={{0,4},{4,8},{8,12},{12,16},{16,20},{20,24},{24,28},{28,0},{1,5},{5... | collective-permute-start | bytes 466952 | tf_op jit(solution)/shard_map/ppermute | solution.py:41
  55.4 2.5 %collective-permute-start.1 = (f32[19,16,1,128]{3,1,2,0:T(8,128)S(1)}, f32[19,16,1,128]{3,1,2,0:T(8,128)S(1)}, u32[]{:S(2)}, u32[]{:S(2)}) collective-permute-start(f32[19,16,1,128]{3,1,2,0:T(8,128)S(1)} %bitcast.404), channel_id=1, source_target_pairs={{4,0},{8,4},{12,8},{16,12},{20,16},{24,20},{28,24},{0,28},{5,1},{9... | collective-permute-start | bytes 466952 | tf_op jit(solution)/shard_map/ppermute | solution.py:44
  57.9 3.3 %collective-permute-done = f32[19,16,1,128]{3,1,2,0:T(8,128)S(1)} collective-permute-done((f32[19,16,1,128]{3,1,2,0:T(8,128)S(1)}, f32[19,16,1,128]{3,1,2,0:T(8,128)S(1)}, u32[]{:S(2)}, u32[]{:S(2)}) %collective-permute-start) | collective-permute-done | bytes 155680 | tf_op jit(solution)/shard_map/ppermute | solution.py:41
  61.2 0.0 copy-start.3
  61.2 1.3 %collective-permute-done.1 = f32[19,16,1,128]{3,1,2,0:T(8,128)S(1)} collective-permute-done((f32[19,16,1,128]{3,1,2,0:T(8,128)S(1)}, f32[19,16,1,128]{3,1,2,0:T(8,128)S(1)}, u32[]{:S(2)}, u32[]{:S(2)}) %collective-permute-start.1) | collective-permute-done | bytes 155680 | tf_op jit(solution)/shard_map/ppermute | solution.py:44
  62.5 0.0 copy-done.3
  62.5 0.5 pad_maximum_fusion
  63.0 3.1 %fusion.174 = (f32[19,16,10,1]{3,2,1,0:T(8,128)}, f32[19,16,10,1]{3,2,1,0:T(8,128)}) fusion(f32[19,16,10,128]{3,2,1,0:T(8,128)S(1)} %pad_maximum_fusion), kind=kLoop, calls=%fused_computation.315 | loop fusion | bytes 48640 | tf_op jit(solution)/shard_map/slice | solution.py:44
  66.1 2.8 %copy.56 = f32[19,16,10,1]{0,1,3,2:T(8,128)S(1)} copy(f32[19,16,10,1]{3,2,1,0:T(8,128)} %get-tuple-element.18) | data formatting | bytes 24320 | tf_op jit(solution)/shard_map/slice | solution.py:42
  68.9 2.1 %collective-permute-start.2 = (f32[19,16,10,1]{0,1,3,2:T(8,128)S(1)}, f32[19,16,10,1]{0,1,3,2:T(8,128)S(1)}, u32[]{:S(2)}, u32[]{:S(2)}) collective-permute-start(f32[19,16,10,1]{0,1,3,2:T(8,128)S(1)} %copy.56), channel_id=1, source_target_pairs={{0,2},{2,0},{1,3},{3,1},{4,6},{6,4},{5,7},{7,5},{8,10},{10,8},{9,1... | collective-permute-start | bytes 36488 | tf_op jit(solution)/shard_map/ppermute | solution.py:41
  71.0 0.6 constant_dynamic-update-slice_fusion.35
  71.6 2.8 %copy.58 = f32[19,16,10,1]{0,1,3,2:T(8,128)S(1)} copy(f32[19,16,10,1]{3,2,1,0:T(8,128)} %get-tuple-element.17) | data formatting | bytes 24320 | tf_op jit(solution)/shard_map/slice | solution.py:44
  74.5 0.1 collective-permute-start.3
  74.5 0.0 collective-permute-done.2
  74.5 3.7 %copy.57 = f32[19,16,10,1]{3,2,1,0:T(8,128)} copy(f32[19,16,10,1]{0,1,3,2:T(8,128)S(1)} %collective-permute-done.2) | data formatting | bytes 24320 | tf_op jit(solution)/shard_map/ppermute | solution.py:41
  78.2 1.6 %constant_dynamic-update-slice_fusion.34 = f32[19,16,8,128]{3,2,1,0:T(8,128)} fusion(f32[19,16,8,128]{3,2,1,0:T(8,128)} %constant_dynamic-update-slice_fusion.35, f32[19,16,10,1]{3,2,1,0:T(8,128)} %copy.57, f32[19,16,1,128]{3,2,1,0:T(1,128)S(1)} %bitcast.387, f32[19,16,8,128]{3,2,1,0:T(8,128)S(1)} %constant_dynamic-update-slice_fusion, ...), kind=kLoop, calls=%fused_computation.63 | loop fusion | flops 49152 | bytes 4112384
  79.9 0.0 collective-permute-done.3
  79.9 3.7 %copy.59 = f32[19,16,10,1]{3,2,1,0:T(8,128)} copy(f32[19,16,10,1]{0,1,3,2:T(8,128)S(1)} %collective-permute-done.3) | data formatting | bytes 24320 | tf_op jit(solution)/shard_map/ppermute | solution.py:44
  83.6 1.8 %pad_maximum_fusion.1 = (f32[19,1,10,130]{3,2,1,0:T(8,128)S(1)}, f32[19,1,10,130]{3,2,1,0:T(8,128)S(1)}) fusion(f32[19,16,10,1]{3,2,1,0:T(8,128)} %copy.59, f32[19,16,10,1]{3,2,1,0:T(8,128)} %copy.57, f32[19,16,1,128]{3,2,1,0:T(1,128)S(1)} %bitcast.388, f32[19,16,8,128]{3,2,1,0:T(8,128)S(1)} %constant_dynamic-update-slice_fusion, ...), kind=kLoop, calls=%fused_computation.3 | loop fusion | flops 197600 | bytes 1778400 | tf_op jit(solution)/shard_map/concatenate | solution.py:45
  85.4 0.1 collective-permute-start.5
  85.4 0.0 copy-start
  85.5 0.5 collective-permute-start.4
  85.9 0.8 constant_dynamic-update-slice_fusion.33
  86.7 0.8 collective-permute-done.4
  87.5 0.7 constant_dynamic-update-slice_fusion.32
  88.2 0.0 collective-permute-done.5
  88.2 0.7 constant_dynamic-update-slice_fusion.31
  88.9 0.7 constant_dynamic-update-slice_fusion.30
  89.7 0.8 constant_dynamic-update-slice_fusion.29
  90.4 0.8 constant_dynamic-update-slice_fusion.28
  91.2 0.8 constant_dynamic-update-slice_fusion.27
  91.9 0.7 constant_dynamic-update-slice_fusion.26
  92.6 0.7 constant_dynamic-update-slice_fusion.25
  93.4 0.7 constant_dynamic-update-slice_fusion.24
  94.1 0.7 constant_dynamic-update-slice_fusion.23
  94.8 0.7 constant_dynamic-update-slice_fusion.22
  95.5 0.8 constant_dynamic-update-slice_fusion.21
  96.3 0.7 constant_dynamic-update-slice_fusion.20
  97.0 0.8 constant_dynamic-update-slice_fusion.19
  (31 shorter events, 0.9 us)
Async XLA Ops:
  2.7 3.2 %copy-start.6 = (s32[1,1,1,512]{3,2,1,0:T(1,128)S(1)}, s32[1,1,1,512]{3,2,1,0:T(1,128)}, u32[]{:S(2)}) copy-start(s32[1,1,1,512]{3,2,1,0:T(1,128)} %param.11) | copy-start | bytes 6148
  2.7 3.2 %copy-start.7 = (f32[1,1,1,512]{3,2,1,0:T(1,128)S(1)}, f32[1,1,1,512]{3,2,1,0:T(1,128)}, u32[]{:S(2)}) copy-start(f32[1,1,1,512]{3,2,1,0:T(1,128)} %param.12) | copy-start | bytes 6148
  2.7 45.4 %copy-start.9 = (s32[40]{0:T(128)S(1)}, s32[40]{0:T(128)}, u32[]{:S(2)}) copy-start(s32[40]{0:T(128)} %param.14) | copy-start | bytes 484
  2.7 45.5 %copy-start.10 = (f32[12]{0:T(128)S(1)}, f32[12]{0:T(128)}, u32[]{:S(2)}) copy-start(f32[12]{0:T(128)} %param.15) | copy-start | bytes 148
  2.7 45.5 %copy-start.5 = (f32[1,1,1,12,512]{4,2,3,1,0:T(1,128)S(1)}, f32[1,1,1,12,512]{4,2,3,1,0:T(1,128)}, u32[]{:S(2)}) copy-start(f32[1,1,1,12,512]{4,2,3,1,0:T(1,128)} %param.13) | copy-start | bytes 73732
  2.8 48.9 %copy-start.2 = (f32[19,16,8,128]{3,2,1,0:T(8,128)S(1)}, f32[19,16,8,128]{3,2,1,0:T(8,128)}, u32[]{:S(2)}) copy-start(f32[19,16,8,128]{3,2,1,0:T(8,128)} %param.8) | copy-start | bytes 3735556
  2.8 48.9 %copy-start.4 = (s32[16,8,128]{2,1,0:T(8,128)S(1)}, s32[16,8,128]{2,1,0:T(8,128)}, u32[]{:S(2)}) copy-start(s32[16,8,128]{2,1,0:T(8,128)} %param.9) | copy-start | bytes 196612
  48.1 3.9 %copy-start.11 = (f32[40]{0:T(128)}, f32[40]{0:T(128)S(1)}, u32[]{:S(2)}) copy-start(f32[40]{0:T(128)S(1)} %psum.7) | copy-start | bytes 484
  48.2 3.7 %copy-start.8 = (f32[12]{0:T(128)}, f32[12]{0:T(128)S(1)}, u32[]{:S(2)}) copy-start(f32[12]{0:T(128)S(1)} %mul.413) | copy-start | bytes 148
  53.1 8.0 %collective-permute-start = (f32[19,16,1,128]{3,1,2,0:T(8,128)S(1)}, f32[19,16,1,128]{3,1,2,0:T(8,128)S(1)}, u32[]{:S(2)}, u32[]{:S(2)}) collective-permute-start(f32[19,16,1,128]{3,1,2,0:T(8,128)S(1)} %bitcast.405), channel_id=1, source_target_pairs={{0,4},{4,8},{8,12},{12,16},{16,20},{20,24},{24,28},{28,0},{1,5},{5... | collective-permute-start | bytes 466952 | tf_op jit(solution)/shard_map/ppermute | solution.py:41
  55.4 7.1 %collective-permute-start.1 = (f32[19,16,1,128]{3,1,2,0:T(8,128)S(1)}, f32[19,16,1,128]{3,1,2,0:T(8,128)S(1)}, u32[]{:S(2)}, u32[]{:S(2)}) collective-permute-start(f32[19,16,1,128]{3,1,2,0:T(8,128)S(1)} %bitcast.404), channel_id=1, source_target_pairs={{4,0},{8,4},{12,8},{16,12},{20,16},{24,20},{28,24},{0,28},{5,1},{9... | collective-permute-start | bytes 466952 | tf_op jit(solution)/shard_map/ppermute | solution.py:44
  61.2 1.4 %copy-start.3 = (f32[19,16,8,128]{3,2,1,0:T(8,128)}, f32[19,16,8,128]{3,2,1,0:T(8,128)S(1)}, u32[]{:S(2)}) copy-start(f32[19,16,8,128]{3,2,1,0:T(8,128)S(1)} %constant_dynamic-update-slice_fusion.36) | copy-start | bytes 3735556
  68.9 5.6 %collective-permute-start.2 = (f32[19,16,10,1]{0,1,3,2:T(8,128)S(1)}, f32[19,16,10,1]{0,1,3,2:T(8,128)S(1)}, u32[]{:S(2)}, u32[]{:S(2)}) collective-permute-start(f32[19,16,10,1]{0,1,3,2:T(8,128)S(1)} %copy.56), channel_id=1, source_target_pairs={{0,2},{2,0},{1,3},{3,1},{4,6},{6,4},{5,7},{7,5},{8,10},{10,8},{9,1... | collective-permute-start | bytes 36488 | tf_op jit(solution)/shard_map/ppermute | solution.py:41
  74.5 5.4 %collective-permute-start.3 = (f32[19,16,10,1]{0,1,3,2:T(8,128)S(1)}, f32[19,16,10,1]{0,1,3,2:T(8,128)S(1)}, u32[]{:S(2)}, u32[]{:S(2)}) collective-permute-start(f32[19,16,10,1]{0,1,3,2:T(8,128)S(1)} %copy.58), channel_id=1, source_target_pairs={{2,0},{0,2},{3,1},{1,3},{6,4},{4,6},{7,5},{5,7},{10,8},{8,10},{11,... | collective-permute-start | bytes 36488 | tf_op jit(solution)/shard_map/ppermute | solution.py:44
  83.6 2.4 %copy-start.1 = (f32[19,16,10,1]{3,2,1,0:T(8,128)S(1)}, f32[19,16,10,1]{3,2,1,0:T(8,128)}, u32[]{:S(2)}) copy-start(f32[19,16,10,1]{3,2,1,0:T(8,128)} %copy.59) | copy-start | bytes 36484
  85.4 2.8 %collective-permute-start.5 = (f32[19,1,10,130]{3,2,1,0:T(8,128)S(1)}, f32[19,1,10,130]{3,2,1,0:T(8,128)S(1)}, u32[]{:S(2)}, u32[]{:S(2)}) collective-permute-start(f32[19,1,10,130]{3,2,1,0:T(8,128)S(1)} %get-tuple-element.15), channel_id=1, source_target_pairs={{1,0},{0,1},{3,2},{2,3},{5,4},{4,5},{7,6},{6,7},{9,8},{8,9},{11,10... | collective-permute-start | bytes 296408 | tf_op jit(solution)/shard_map/ppermute | solution.py:44
  85.4 2.0 %copy-start = (f32[19,16,10,1]{3,2,1,0:T(8,128)S(1)}, f32[19,16,10,1]{3,2,1,0:T(8,128)}, u32[]{:S(2)}) copy-start(f32[19,16,10,1]{3,2,1,0:T(8,128)} %copy.57) | copy-start | bytes 36484
  85.5 2.0 %collective-permute-start.4 = (f32[19,1,10,130]{3,2,1,0:T(8,128)S(1)}, f32[19,1,10,130]{3,2,1,0:T(8,128)S(1)}, u32[]{:S(2)}, u32[]{:S(2)}) collective-permute-start(f32[19,1,10,130]{3,2,1,0:T(8,128)S(1)} %get-tuple-element.16), channel_id=1, source_target_pairs={{0,1},{1,0},{2,3},{3,2},{4,5},{5,4},{6,7},{7,6},{8,9},{9,8},{10,11... | collective-permute-start | bytes 296408 | tf_op jit(solution)/shard_map/ppermute | solution.py:41
where the time goes:
time: 98.2 us; the launch traced here: 97.8 us
  blocking collectives  42 us (43%)
  other arithmetic  22.3 us (23%)
  local copies, waits for them, and re-layouts  19.7 us (20%)
  starting transfers between devices  7.45 us (8%)
  waiting for transfers between devices  5.39 us (5%)
  between operations  0.99 us (1%)
    psum x1, blocking collectives, per_device(): panel_force = lax.psum(partial_force, ('gx', 'gy', 'gz'))  42 us
    unnamed x34, other arithmetic  13.4 us
    slice x3, local copies, waits for them, and re-layouts, padded_2(): lax.slice_in_dim(block, 0, width, axis=dim)  6.12 us
    ppermute x3, starting transfers between devices, padded_2(): lax.ppermute(lax.slice_in_dim(block, block.shape[dim] - width, None, axis...  4.86 us
    ppermute x3, waiting for transfers between devices, padded_2(): lax.ppermute(lax.slice_in_dim(block, block.shape[dim] - width, None, axis...  4.05 us
    ppermute x1, local copies, waits for them, and re-layouts, padded_2(): lax.ppermute(lax.slice_in_dim(block, block.shape[dim] - width, None, axis...  3.71 us
    ppermute x1, local copies, waits for them, and re-layouts, padded_2(): lax.ppermute(lax.slice_in_dim(block, 0, width, axis=dim), axis, backward)  3.7 us
    scatter-add x1, other arithmetic, per_device(): jnp.zeros_like(flat_density).at[cell_list].add(values)  3.28 us
  transfers between devices with their start and end apart: 6, of which 3 were waited for; matrix products, arithmetic and copies ran while one was open for 11% of the time, Pallas kernels for 0%

commit v1 on v0

--- a/solution.py
+++ b/solution.py
@@ -117,7 +117,7 @@
     partial_force = jnp.sum(
         jnp.where(panel_list[:, None] == panel_ids[None, :], contrib[:, None], 0.0), axis=0
     )
-    panel_force = lax.psum(partial_force, ("gx", "gy", "gz"))
+    panel_force = jax.lax.psum(jax.lax.psum(partial_force, ("gy", "gz")), "gx")
     mode_ids = jnp.arange(MODES, dtype=jnp.int32)
     mode_load = jnp.sum(
         jnp.where(mode_of_panel[:, None] == mode_ids[None, :], panel_force[:, None], 0.0), axis=0

time: 98.2 us -> 85.7 us (0.87)
  blocking collectives: 42 us -> 30 us
  waiting for transfers between devices: 5.39 us -> 4 us
    psum x1 -> x2, blocking collectives: 42 us -> 30 us  [per_device(): panel_force = jax.lax.psum(jax.lax.psum(partial_force, ('gy', 'gz')), 'gx')]
    ppermute x3, starting transfers between devices: 4.86 us -> 1.09 us  [padded_2(): lax.ppermute(lax.slice_in_dim(block, block.shape[dim] - width, None, axis...]
    ppermute x3, starting transfers between devices: 2.58 us -> 6.35 us  [padded_2(): lax.ppermute(lax.slice_in_dim(block, 0, width, axis=dim), axis, backward)]
    ppermute x3, waiting for transfers between devices: 1.34 us -> 0.01 us  [padded_2(): lax.ppermute(lax.slice_in_dim(block, 0, width, axis=dim), axis, backward)]
    unnamed x26, local copies, waits for them, and re-layouts: 0.18 us -> 1.19 us
  transfers between devices with their start and end apart: 6 -> 6, of which waited for: 3 -> 2; matrix products, arithmetic and copies ran while one was open for 11% -> 12% of each run, Pallas kernels for 0% -> 0%
where the time goes in v1:
time: 85.7 us; the launch traced here: 85.4 us
  blocking collectives  30 us (35%)
  other arithmetic  22.3 us (26%)
  local copies, waits for them, and re-layouts  20.6 us (24%)
  starting transfers between devices  7.43 us (9%)
  waiting for transfers between devices  4 us (5%)
  between operations  1 us (1%)
    psum x2, blocking collectives, per_device(): panel_force = jax.lax.psum(jax.lax.psum(partial_force, ('gy', 'gz')), 'gx')  30 us
    unnamed x34, other arithmetic  13.4 us
    ppermute x3, starting transfers between devices, padded_2(): lax.ppermute(lax.slice_in_dim(block, 0, width, axis=dim), axis, backward)  6.35 us
    slice x3, local copies, waits for them, and re-layouts, padded_2(): lax.slice_in_dim(block, 0, width, axis=dim)  6.09 us
    ppermute x3, waiting for transfers between devices, padded_2(): lax.ppermute(lax.slice_in_dim(block, block.shape[dim] - width, None, axis...  3.99 us
    ppermute x1, local copies, waits for them, and re-layouts, padded_2(): lax.ppermute(lax.slice_in_dim(block, 0, width, axis=dim), axis, backward)  3.69 us
    ppermute x1, local copies, waits for them, and re-layouts, padded_2(): lax.ppermute(lax.slice_in_dim(block, block.shape[dim] - width, None, axis...  3.68 us
    scatter-add x1, other arithmetic, per_device(): jnp.zeros_like(flat_density).at[cell_list].add(values)  3.28 us
  transfers between devices with their start and end apart: 6, of which 2 were waited for; matrix products, arithmetic and copies ran while one was open for 12% of the time, Pallas kernels for 0%

profile of v1, /device:TPU:0, one launch (start us, length us, event | category | flops | bytes accessed | tf_op | source)
XLA Modules:
  0.0 85.4 jit_solution(3776098645596406487)
XLA Ops:
  0.6 0.7 compare_select_fusion
  1.3 1.4 %bitcast_add_fusion = f32[16384]{0:T(1024)S(1)} fusion(f32[19,16,8,128]{3,2,1,0:T(8,128)} %param.8), kind=kLoop, calls=%fused_computation.249 | loop fusion | flops 294912 | bytes 1310720 | tf_op jit(solution)/shard_map/add | solution.py:52
  2.7 0.0 copy-start.6
  2.7 0.0 copy-start.7
  2.7 0.0 copy-start.9
  2.7 0.0 copy-start.10
  2.7 0.0 copy-start.5
  2.8 0.0 copy-start.2
  2.8 0.0 copy-start.4
  2.8 3.1 %gather_fusion = f32[512]{0:T(512)S(1)} fusion(f32[16384]{0:T(1024)S(1)} %bitcast_add_fusion, s32[1024]{0:T(1024)S(1)} %pad_clamp_fusion), kind=kCustom, calls=%fused_computation | custom fusion | bytes 6144 | tf_op jit(solution)/shard_map/gather | solution.py:113
  5.9 0.0 copy-done.6
  5.9 0.0 copy-done.7
  6.0 0.1 select_reduce_fusion
  6.1 8.3 %psum.14 = f32[40]{0:T(128)S(1)} all-reduce(f32[40]{0:T(128)S(1)} %select_reduce_fusion), channel_id=1, replica_groups=mesh['gx'=8,'gy'=2,'gz'=2] {'gy','gz'}, use_global_device_ids=true, to_apply=%region_1.2 | all-reduce | flops 40 | bytes 320 | tf_op jit(solution)/shard_map/psum | solution.py:120
  14.4 21.7 %psum.15 = f32[40]{0:T(128)S(1)} all-reduce(f32[40]{0:T(128)S(1)} %psum.14), channel_id=1, replica_groups=mesh['gx'=8,'gy'=2,'gz'=2] {'gx'}, use_global_device_ids=true, to_apply=%region_2.3 | all-reduce | flops 40 | bytes 320 | tf_op jit(solution)/shard_map/psum | solution.py:120
  36.1 0.0 copy-done.9
  36.1 0.1 select_reduce_fusion.1
  36.2 0.0 copy-done.10
  36.2 0.0 copy-done.5
  36.2 0.0 copy-start.8
  36.2 0.1 fusion.168
  36.3 3.3 %scatter_custom_fusion = f32[16384]{0:T(1024)S(1)} fusion(s32[512]{0:T(512)S(1)} %bitcast.409, f32[512]{0:T(512)S(1)} %multiply_select_fusion, f32[]{:T(128)} %constant.4.clone.1), kind=kCustom, calls=%fused_computation.305 | custom fusion | flops 512 | bytes 65540 | tf_op jit(solution)/shard_map/scatter-add | solution.py:129
  39.6 0.0 copy-done.2
  39.6 0.2 fusion.1
  39.8 0.1 copy.82
  40.9 0.2 fusion.175
  41.1 0.1 collective-permute-start
  41.2 4.7 %collective-permute-start.1 = (f32[19,16,1,128]{3,1,2,0:T(8,128)S(1)}, f32[19,16,1,128]{3,1,2,0:T(8,128)S(1)}, u32[]{:S(2)}, u32[]{:S(2)}) collective-permute-start(f32[19,16,1,128]{3,1,2,0:T(8,128)S(1)} %bitcast.404), channel_id=1, source_target_pairs={{4,0},{8,4},{12,8},{16,12},{20,16},{24,20},{28,24},{0,28},{5,1},{9... | collective-permute-start | bytes 466952 | tf_op jit(solution)/shard_map/ppermute | solution.py:44
  45.9 3.2 %collective-permute-done = f32[19,16,1,128]{3,1,2,0:T(8,128)S(1)} collective-permute-done((f32[19,16,1,128]{3,1,2,0:T(8,128)S(1)}, f32[19,16,1,128]{3,1,2,0:T(8,128)S(1)}, u32[]{:S(2)}, u32[]{:S(2)}) %collective-permute-start) | collective-permute-done | bytes 155680 | tf_op jit(solution)/shard_map/ppermute | solution.py:41
  49.1 0.0 copy-start.3
  49.1 0.0 collective-permute-done.1
  49.1 1.0 %copy-done.3 = f32[19,16,8,128]{3,2,1,0:T(8,128)} copy-done((f32[19,16,8,128]{3,2,1,0:T(8,128)}, f32[19,16,8,128]{3,2,1,0:T(8,128)S(1)}, u32[]{:S(2)}) %copy-start.3) | copy-done | bytes 1245208
  50.1 0.5 pad_maximum_fusion
  50.6 3.1 %fusion.174 = (f32[19,16,10,1]{3,2,1,0:T(8,128)}, f32[19,16,10,1]{3,2,1,0:T(8,128)}) fusion(f32[19,16,10,128]{3,2,1,0:T(8,128)S(1)} %pad_maximum_fusion), kind=kLoop, calls=%fused_computation.315 | loop fusion | bytes 48640 | tf_op jit(solution)/shard_map/slice | solution.py:44
  53.7 2.8 %copy.56 = f32[19,16,10,1]{0,1,3,2:T(8,128)S(1)} copy(f32[19,16,10,1]{3,2,1,0:T(8,128)} %get-tuple-element.18) | data formatting | bytes 24320 | tf_op jit(solution)/shard_map/slice | solution.py:42
  56.5 0.5 collective-permute-start.2
  57.1 0.6 constant_dynamic-update-slice_fusion.35
  57.7 2.8 %copy.58 = f32[19,16,10,1]{0,1,3,2:T(8,128)S(1)} copy(f32[19,16,10,1]{3,2,1,0:T(8,128)} %get-tuple-element.17) | data formatting | bytes 24320 | tf_op jit(solution)/shard_map/slice | solution.py:44
  60.5 1.6 %collective-permute-start.3 = (f32[19,16,10,1]{0,1,3,2:T(8,128)S(1)}, f32[19,16,10,1]{0,1,3,2:T(8,128)S(1)}, u32[]{:S(2)}, u32[]{:S(2)}) collective-permute-start(f32[19,16,10,1]{0,1,3,2:T(8,128)S(1)} %copy.58), channel_id=1, source_target_pairs={{2,0},{0,2},{3,1},{1,3},{6,4},{4,6},{7,5},{5,7},{10,8},{8,10},{11,... | collective-permute-start | bytes 36488 | tf_op jit(solution)/shard_map/ppermute | solution.py:44
  62.1 0.0 collective-permute-done.2
  62.1 3.7 %copy.57 = f32[19,16,10,1]{3,2,1,0:T(8,128)} copy(f32[19,16,10,1]{0,1,3,2:T(8,128)S(1)} %collective-permute-done.2) | data formatting | bytes 24320 | tf_op jit(solution)/shard_map/ppermute | solution.py:41
  65.8 1.6 %constant_dynamic-update-slice_fusion.34 = f32[19,16,8,128]{3,2,1,0:T(8,128)} fusion(f32[19,16,8,128]{3,2,1,0:T(8,128)} %constant_dynamic-update-slice_fusion.35, f32[19,16,10,1]{3,2,1,0:T(8,128)} %copy.57, f32[19,16,1,128]{3,2,1,0:T(1,128)S(1)} %bitcast.387, f32[19,16,8,128]{3,2,1,0:T(8,128)S(1)} %constant_dynamic-update-slice_fusion, ...), kind=kLoop, calls=%fused_computation.63 | loop fusion | flops 49152 | bytes 4112384
  67.4 0.0 collective-permute-done.3
  67.4 3.7 %copy.59 = f32[19,16,10,1]{3,2,1,0:T(8,128)} copy(f32[19,16,10,1]{0,1,3,2:T(8,128)S(1)} %collective-permute-done.3) | data formatting | bytes 24320 | tf_op jit(solution)/shard_map/ppermute | solution.py:44
  71.1 1.8 %pad_maximum_fusion.1 = (f32[19,1,10,130]{3,2,1,0:T(8,128)S(1)}, f32[19,1,10,130]{3,2,1,0:T(8,128)S(1)}) fusion(f32[19,16,10,1]{3,2,1,0:T(8,128)} %copy.59, f32[19,16,10,1]{3,2,1,0:T(8,128)} %copy.57, f32[19,16,1,128]{3,2,1,0:T(1,128)S(1)} %bitcast.388, f32[19,16,8,128]{3,2,1,0:T(8,128)S(1)} %constant_dynamic-update-slice_fusion, ...), kind=kLoop, calls=%fused_computation.3 | loop fusion | flops 197600 | bytes 1778400 | tf_op jit(solution)/shard_map/concatenate | solution.py:45
  72.9 0.1 collective-permute-start.5
  73.0 0.5 collective-permute-start.4
  73.5 0.8 constant_dynamic-update-slice_fusion.33
  74.2 0.8 collective-permute-done.4
  75.0 0.7 constant_dynamic-update-slice_fusion.32
  75.7 0.0 collective-permute-done.5
  75.8 0.7 constant_dynamic-update-slice_fusion.31
  76.5 0.7 constant_dynamic-update-slice_fusion.30
  77.2 0.8 constant_dynamic-update-slice_fusion.29
  78.0 0.8 constant_dynamic-update-slice_fusion.28
  78.7 0.8 constant_dynamic-update-slice_fusion.27
  79.5 0.7 constant_dynamic-update-slice_fusion.26
  80.2 0.7 constant_dynamic-update-slice_fusion.25
  80.9 0.7 constant_dynamic-update-slice_fusion.24
  81.6 0.7 constant_dynamic-update-slice_fusion.23
  82.4 0.7 constant_dynamic-update-slice_fusion.22
  83.1 0.8 constant_dynamic-update-slice_fusion.21
  83.9 0.7 constant_dynamic-update-slice_fusion.20
  84.6 0.8 constant_dynamic-update-slice_fusion.19
  (32 shorter events, 0.9 us)
Async XLA Ops:
  2.7 3.2 %copy-start.6 = (s32[1,1,1,512]{3,2,1,0:T(1,128)S(1)}, s32[1,1,1,512]{3,2,1,0:T(1,128)}, u32[]{:S(2)}) copy-start(s32[1,1,1,512]{3,2,1,0:T(1,128)} %param.11) | copy-start | bytes 6148
  2.7 3.2 %copy-start.7 = (f32[1,1,1,512]{3,2,1,0:T(1,128)S(1)}, f32[1,1,1,512]{3,2,1,0:T(1,128)}, u32[]{:S(2)}) copy-start(f32[1,1,1,512]{3,2,1,0:T(1,128)} %param.12) | copy-start | bytes 6148
  2.7 33.4 %copy-start.9 = (s32[40]{0:T(128)S(1)}, s32[40]{0:T(128)}, u32[]{:S(2)}) copy-start(s32[40]{0:T(128)} %param.14) | copy-start | bytes 484
  2.7 33.5 %copy-start.10 = (f32[12]{0:T(128)S(1)}, f32[12]{0:T(128)}, u32[]{:S(2)}) copy-start(f32[12]{0:T(128)} %param.15) | copy-start | bytes 148
  2.7 33.5 %copy-start.5 = (f32[1,1,1,12,512]{4,2,3,1,0:T(1,128)S(1)}, f32[1,1,1,12,512]{4,2,3,1,0:T(1,128)}, u32[]{:S(2)}) copy-start(f32[1,1,1,12,512]{4,2,3,1,0:T(1,128)} %param.13) | copy-start | bytes 73732
  2.8 36.9 %copy-start.2 = (f32[19,16,8,128]{3,2,1,0:T(8,128)S(1)}, f32[19,16,8,128]{3,2,1,0:T(8,128)}, u32[]{:S(2)}) copy-start(f32[19,16,8,128]{3,2,1,0:T(8,128)} %param.8) | copy-start | bytes 3735556
  2.8 36.9 %copy-start.4 = (s32[16,8,128]{2,1,0:T(8,128)S(1)}, s32[16,8,128]{2,1,0:T(8,128)}, u32[]{:S(2)}) copy-start(s32[16,8,128]{2,1,0:T(8,128)} %param.9) | copy-start | bytes 196612
  36.1 3.9 %copy-start.11 = (f32[40]{0:T(128)}, f32[40]{0:T(128)S(1)}, u32[]{:S(2)}) copy-start(f32[40]{0:T(128)S(1)} %psum.15) | copy-start | bytes 484
  36.2 3.7 %copy-start.8 = (f32[12]{0:T(128)}, f32[12]{0:T(128)S(1)}, u32[]{:S(2)}) copy-start(f32[12]{0:T(128)S(1)} %mul.413) | copy-start | bytes 148
  41.1 8.0 %collective-permute-start = (f32[19,16,1,128]{3,1,2,0:T(8,128)S(1)}, f32[19,16,1,128]{3,1,2,0:T(8,128)S(1)}, u32[]{:S(2)}, u32[]{:S(2)}) collective-permute-start(f32[19,16,1,128]{3,1,2,0:T(8,128)S(1)} %bitcast.405), channel_id=1, source_target_pairs={{0,4},{4,8},{8,12},{12,16},{16,20},{20,24},{24,28},{28,0},{1,5},{5... | collective-permute-start | bytes 466952 | tf_op jit(solution)/shard_map/ppermute | solution.py:41
  41.2 7.9 %collective-permute-start.1 = (f32[19,16,1,128]{3,1,2,0:T(8,128)S(1)}, f32[19,16,1,128]{3,1,2,0:T(8,128)S(1)}, u32[]{:S(2)}, u32[]{:S(2)}) collective-permute-start(f32[19,16,1,128]{3,1,2,0:T(8,128)S(1)} %bitcast.404), channel_id=1, source_target_pairs={{4,0},{8,4},{12,8},{16,12},{20,16},{24,20},{28,24},{0,28},{5,1},{9... | collective-permute-start | bytes 466952 | tf_op jit(solution)/shard_map/ppermute | solution.py:44
  49.1 1.0 %copy-start.3 = (f32[19,16,8,128]{3,2,1,0:T(8,128)}, f32[19,16,8,128]{3,2,1,0:T(8,128)S(1)}, u32[]{:S(2)}) copy-start(f32[19,16,8,128]{3,2,1,0:T(8,128)S(1)} %constant_dynamic-update-slice_fusion.36) | copy-start | bytes 3735556
  56.5 5.6 %collective-permute-start.2 = (f32[19,16,10,1]{0,1,3,2:T(8,128)S(1)}, f32[19,16,10,1]{0,1,3,2:T(8,128)S(1)}, u32[]{:S(2)}, u32[]{:S(2)}) collective-permute-start(f32[19,16,10,1]{0,1,3,2:T(8,128)S(1)} %copy.56), channel_id=1, source_target_pairs={{0,2},{2,0},{1,3},{3,1},{4,6},{6,4},{5,7},{7,5},{8,10},{10,8},{9,1... | collective-permute-start | bytes 36488 | tf_op jit(solution)/shard_map/ppermute | solution.py:41
  60.5 6.9 %collective-permute-start.3 = (f32[19,16,10,1]{0,1,3,2:T(8,128)S(1)}, f32[19,16,10,1]{0,1,3,2:T(8,128)S(1)}, u32[]{:S(2)}, u32[]{:S(2)}) collective-permute-start(f32[19,16,10,1]{0,1,3,2:T(8,128)S(1)} %copy.58), channel_id=1, source_target_pairs={{2,0},{0,2},{3,1},{1,3},{6,4},{4,6},{7,5},{5,7},{10,8},{8,10},{11,... | collective-permute-start | bytes 36488 | tf_op jit(solution)/shard_map/ppermute | solution.py:44
  71.1 2.4 %copy-start.1 = (f32[19,16,10,1]{3,2,1,0:T(8,128)S(1)}, f32[19,16,10,1]{3,2,1,0:T(8,128)}, u32[]{:S(2)}) copy-start(f32[19,16,10,1]{3,2,1,0:T(8,128)} %copy.59) | copy-start | bytes 36484
  72.9 2.8 %collective-permute-start.5 = (f32[19,1,10,130]{3,2,1,0:T(8,128)S(1)}, f32[19,1,10,130]{3,2,1,0:T(8,128)S(1)}, u32[]{:S(2)}, u32[]{:S(2)}) collective-permute-start(f32[19,1,10,130]{3,2,1,0:T(8,128)S(1)} %get-tuple-element.15), channel_id=1, source_target_pairs={{1,0},{0,1},{3,2},{2,3},{5,4},{4,5},{7,6},{6,7},{9,8},{8,9},{11,10... | collective-permute-start | bytes 296408 | tf_op jit(solution)/shard_map/ppermute | solution.py:44
  73.0 2.0 %copy-start = (f32[19,16,10,1]{3,2,1,0:T(8,128)S(1)}, f32[19,16,10,1]{3,2,1,0:T(8,128)}, u32[]{:S(2)}) copy-start(f32[19,16,10,1]{3,2,1,0:T(8,128)} %copy.57) | copy-start | bytes 36484
  73.0 2.0 %collective-permute-start.4 = (f32[19,1,10,130]{3,2,1,0:T(8,128)S(1)}, f32[19,1,10,130]{3,2,1,0:T(8,128)S(1)}, u32[]{:S(2)}, u32[]{:S(2)}) collective-permute-start(f32[19,1,10,130]{3,2,1,0:T(8,128)S(1)} %get-tuple-element.16), channel_id=1, source_target_pairs={{0,1},{1,0},{2,3},{3,2},{4,5},{5,4},{6,7},{7,6},{8,9},{9,8},{10,11... | collective-permute-start | bytes 296408 | tf_op jit(solution)/shard_map/ppermute | solution.py:41
